TPU v7x, 128 devices: a whole 4x4x4 slice. The times are simulated.
128 devices in a mesh: row: 8 (over y_lo, z), col: 16 (over y_hi, x, core).
Axes of the slice: x: 4, y: 4 (y_hi: 2, y_lo: 2; y = y_hi * 2 + y_lo), z: 4, core: 2. Of those that a mesh axis runs over, the one named last changes fastest.
Arguments:
- eigvecs: float32 [65536, 4096], P(('row', 'col')), may hold values from -6 to 6
- panels: float32 [3, 256, 65536], P(None, None, ('row', 'col')), may hold values from -0.09375 to 0.09375
- tri_factors: float32 [3, 256, 256], replicated, may hold values from -0.2 to 0.6, as said below
Outputs:
- back: float32 [65536, 4096], P('row', 'col')
Inputs may be any that keep to these rules, and one draw needn't show every extreme that they name: `tri_factors`: each factor is upper triangular; diagonal entries lie in 0.2 to 0.6.
All inputs are finite; a program needn't handle non-finite values.
Results may differ from a plain program's by a relative error of at most 0.00013.
Values sent between devices are 32-bit elements; how exact they have to be, the bound alone decides.
No kernel may reach another device: no remote copies, remote signals or barrier semaphores. Data moves between devices by JAX's collectives and lax.ppermute only.
A program may use at most 128 MiB of HBM per device.

v0:
```python
import jax
import jax.numpy as jnp
from jax import lax
from jax.sharding import PartitionSpec as P


def product(left, right):
    return jnp.dot(left, right, precision=lax.Precision.HIGHEST, preferred_element_type=jnp.float32)


def spread(panel_t, right):
    return lax.dot_general(
        panel_t,
        right,
        (((0,), (0,)), ((), ())),
        precision=lax.Precision.HIGHEST,
        preferred_element_type=jnp.float32,
    )


def shaped(raw, start, offset):
    count = raw.shape[0]
    width = raw.shape[1]
    place = start + lax.broadcasted_iota(jnp.int32, (count, width), 1)
    limit = offset + lax.broadcasted_iota(jnp.int32, (count, width), 0)
    return jnp.where(
        place < limit, jnp.float32(0.0), jnp.where(place == limit, jnp.float32(1.0), raw)
    )


def apply_chain(block, vectors, tri_factors, total_single):
    for index in reversed(range(len(vectors))):
        w_block = total_single(product(vectors[index], block))
        block = block - spread(vectors[index], product(tri_factors[index], w_block))
    return block


def tile_single(values):
    return lax.psum(values, "row")


def on_device(eigvecs, panels, tri_factors):
    block_size = tri_factors.shape[1]
    count = tri_factors.shape[0]
    tiles = lax.all_to_all(eigvecs, "col", split_axis=1, concat_axis=0, tiled=True)
    gathered = lax.all_gather(panels, "col", axis=2, tiled=True)
    start = lax.axis_index("row") * tiles.shape[0]
    vectors = [shaped(gathered[index], start, (index + 1) * block_size) for index in range(count)]
    return apply_chain(tiles, vectors, tri_factors, tile_single)


def solution(mesh):
    in_specs = (P(("row", "col"), None), P(None, None, ("row", "col")), P())
    out_specs = P("row", "col")
    return jax.shard_map(
        on_device, mesh=mesh, in_specs=in_specs, out_specs=out_specs, check_vma=False
    )
```

profile of v0, /device:TPU:0, one launch (start us, length us, event | category | flops | bytes accessed | tf_op | source)
XLA Modules:
  0.0 585.3 jit_solution(4360634410430133219)
XLA Ops:
  6.5 0.0 all-gather.2.cloned.1.call-start
  6.5 0.7 all-gather.2.cloned.1.call-update
  7.3 7.7 %copy.7 = f32[64,16,8,256]{3,2,0,1:T(8,128)} copy(f32[64,16,8,256]{3,2,1,0:T(8,128)} %bitcast.50) | data formatting | bytes 16777216 | tf_op jit(solution)/shard_map/all_to_all | solution.py:45
  14.9 7.2 %all-to-all-start = ((f32[512,16,256]{2,0,1:T(8,128)}), f32[512,16,256]{2,0,1:T(8,128)}, u32[]{:S(2)}, u32[]{:S(2)}) async-start(f32[512,16,256]{2,0,1:T(8,128)} %bitcast.49), calls=%async_computation | async-start | bytes 16777216 | tf_op jit(solution)/shard_map/all_to_all | solution.py:45
  22.1 0.0 all-reduce.4.cloned.1.call-start
  22.2 127.0 %all-to-all-done = f32[512,16,256]{2,0,1:T(8,128)} async-done(((f32[512,16,256]{2,0,1:T(8,128)}), f32[512,16,256]{2,0,1:T(8,128)}, u32[]{:S(2)}, u32[]{:S(2)}) %all-to-all-start) | async-done | bytes 8388640 | tf_op jit(solution)/shard_map/all_to_all | solution.py:45
  149.2 104.7 %all-gather.2.cloned.1.call-done = f32[3,256,8192]{2,1,0:T(8,128)} async-done(((f32[3,256,512]{2,1,0:T(8,128)}), f32[3,256,8192]{2,1,0:T(8,128)}) %all-gather.2.cloned.1.call-update) | async-done | bytes 25165840 | tf_op jit(solution)/shard_map/all_gather | solution.py:46
  253.9 0.0 copy-start.2
  253.9 14.9 %fusion.4 = f32[256,256]{1,0:T(8,128)} fusion(f32[8192,256]{1,0:T(8,128)} %bitcast.1, f32[3,256,8192]{2,1,0:T(8,128)} %all-gather.2.cloned.1.call-done, s32[8192]{0:T(1024)S(1)} %iota_add_fusion, s32[256]{0:T(256)S(1)} %iota_add_fusion.3), kind=kOutput, calls=%fused_computation.10 | convolution fusion | flops 6450839552 | bytes 17073152 | tf_op jit(solution)/shard_map/dot_general | solution.py:8
  268.8 0.0 all-reduce.4.cloned.1.call-update
  268.8 0.0 all-reduce.6.cloned.1.call-start
  268.9 72.0 %all-reduce.4.cloned.1.call-done = f32[256,256]{1,0:T(8,128)} async-done(((f32[256,256]{1,0:T(8,128)}), f32[256,256]{1,0:T(8,128)}) %all-reduce.4.cloned.1.call-update) | async-done | bytes 262160 | tf_op jit(solution)/shard_map/psum | solution.py:39
  340.8 0.0 copy-done.2
  340.8 1.5 fusion.50
  342.4 17.6 %convolution_subtract_fusion.2 = f32[8192,256]{1,0:T(8,128)S(1)} fusion(f32[8192,256]{1,0:T(8,128)} %bitcast.1, f32[256,256]{1,0:T(8,128)S(1)} %fusion.50, f32[3,256,8192]{2,1,0:T(8,128)} %all-gather.2.cloned.1.call-done, s32[8192]{0:T(1024)S(1)} %iota_add_fusion, s32[256]{0:T(256)S(1)} %iota_add_fusion.3), kind=kOutput, calls=%fused_computation.2 | convolution fusion | flops 6452936704 | bytes 25461760 | tf_op jit(solution)/shard_map/dot_general | solution.py:12
  360.0 0.0 copy-start
  360.1 3.4 copy-done
  363.4 12.3 %fusion.17 = f32[256,256]{1,0:T(8,128)} fusion(f32[8192,256]{1,0:T(8,128)S(1)} %convolution_subtract_fusion.2, f32[3,256,8192]{2,1,0:T(8,128)} %all-gather.2.cloned.1.call-done, s32[8192]{0:T(1024)S(1)} %iota_add_fusion, s32[256]{0:T(256)S(1)} %iota_add_fusion.2), kind=kOutput, calls=%fused_computation.22 | convolution fusion | flops 6450839552 | bytes 17073152 | tf_op jit(solution)/shard_map/dot_general | solution.py:8
  375.8 0.0 all-reduce.6.cloned.1.call-update
  375.8 0.2 all-reduce.8.cloned.1.call-start
  376.0 73.5 %all-reduce.6.cloned.1.call-done = f32[256,256]{1,0:T(8,128)} async-done(((f32[256,256]{1,0:T(8,128)}), f32[256,256]{1,0:T(8,128)}) %all-reduce.6.cloned.1.call-update) | async-done | bytes 262160 | tf_op jit(solution)/shard_map/psum | solution.py:39
  449.5 1.5 fusion.48
  451.0 17.2 %convolution_subtract_fusion.1 = f32[8192,256]{1,0:T(8,128)S(1)} fusion(f32[8192,256]{1,0:T(8,128)} %copy-done, f32[256,256]{1,0:T(8,128)S(1)} %fusion.48, f32[3,256,8192]{2,1,0:T(8,128)} %all-gather.2.cloned.1.call-done, s32[8192]{0:T(1024)S(1)} %iota_add_fusion, s32[256]{0:T(256)S(1)} %iota_add_fusion.2), kind=kOutput, calls=%fused_computation.1 | convolution fusion | flops 6452936704 | bytes 25461760 | tf_op jit(solution)/shard_map/dot_general | solution.py:12
  468.2 0.0 copy-start.1
  468.2 3.4 copy-done.1
  471.6 12.5 %fusion.20 = f32[256,256]{1,0:T(8,128)} fusion(f32[8192,256]{1,0:T(8,128)S(1)} %convolution_subtract_fusion.1, f32[3,256,8192]{2,1,0:T(8,128)} %all-gather.2.cloned.1.call-done, s32[8192]{0:T(1024)S(1)} %iota_add_fusion, s32[256]{0:T(256)S(1)} %iota_add_fusion.1), kind=kOutput, calls=%fused_computation.23 | convolution fusion | flops 6450839552 | bytes 17073152 | tf_op jit(solution)/shard_map/dot_general | solution.py:8
  484.1 0.0 all-reduce.8.cloned.1.call-update
  484.1 73.7 %all-reduce.8.cloned.1.call-done = f32[256,256]{1,0:T(8,128)} async-done(((f32[256,256]{1,0:T(8,128)}), f32[256,256]{1,0:T(8,128)}) %all-reduce.8.cloned.1.call-update) | async-done | bytes 262160 | tf_op jit(solution)/shard_map/psum | solution.py:39
  557.8 1.5 fusion.46
  559.4 19.2 %convolution_subtract_fusion = f32[8192,256]{1,0:T(8,128)} fusion(f32[8192,256]{1,0:T(8,128)} %copy-done.1, f32[256,256]{1,0:T(8,128)S(1)} %fusion.46, f32[3,256,8192]{2,1,0:T(8,128)} %all-gather.2.cloned.1.call-done, s32[8192]{0:T(1024)S(1)} %iota_add_fusion, s32[256]{0:T(256)S(1)} %iota_add_fusion.1), kind=kOutput, calls=%fused_computation | convolution fusion | flops 6452936704 | bytes 25461760 | tf_op jit(solution)/shard_map/dot_general | solution.py:12
  (4 shorter events, 0.0 us)
Async XLA Ops:
  6.5 247.3 %all-gather.2.cloned.1.call-start = ((), (), s32[]{:S(2)}) async-start(), calls=%async_computation.1 | async-start | bytes 26738688 | tf_op jit(solution)/shard_map/all_gather | solution.py:46
  14.9 134.3 %all-to-all-start = ((f32[512,16,256]{2,0,1:T(8,128)}), f32[512,16,256]{2,0,1:T(8,128)}, u32[]{:S(2)}, u32[]{:S(2)}) async-start(f32[512,16,256]{2,0,1:T(8,128)} %bitcast.49), calls=%async_computation | async-start | bytes 16777216 | tf_op jit(solution)/shard_map/all_to_all | solution.py:45
  22.1 318.7 %all-reduce.4.cloned.1.call-start = ((), (), s32[]{:S(2)}) async-start(), calls=%async_computation.2 | async-start | bytes 524288 | tf_op jit(solution)/shard_map/psum | solution.py:39
  253.9 87.0 %copy-start.2 = (f32[3,256,256]{2,1,0:T(8,128)S(1)}, f32[3,256,256]{2,1,0:T(8,128)}, u32[]{:S(2)}) copy-start(f32[3,256,256]{2,1,0:T(8,128)} %param.5) | copy-start | bytes 2359300
  268.8 180.7 %all-reduce.6.cloned.1.call-start = ((), (), s32[]{:S(2)}) async-start(), calls=%async_computation.3 | async-start | bytes 524288 | tf_op jit(solution)/shard_map/psum | solution.py:39
  360.0 3.4 copy-start
  375.8 182.1 %all-reduce.8.cloned.1.call-start = ((), (), s32[]{:S(2)}) async-start(), calls=%async_computation.4 | async-start | bytes 524288 | tf_op jit(solution)/shard_map/psum | solution.py:39
  468.2 3.4 copy-start.1
Sparse Core Ops, SparseCore 0:
  9.8 243.9 all-gather.1
  268.9 71.8 all-reduce.3
  375.9 73.5 all-reduce.5
  484.3 73.5 all-reduce.7
where the time goes:
time: 591 us; the launch traced here: 585 us
  waiting for transfers between devices  452 us (76%)
  matrix products  98.3 us (17%)
  local copies, waits for them, and re-layouts  14.5 us (2%)
  between operations  13.5 us (2%)
  starting transfers between devices  7.47 us (1%)
    psum x3, waiting for transfers between devices, tile_single(): return lax.psum(values, 'row')  219 us
    all_to_all x1, waiting for transfers between devices, on_device(): lax.all_to_all(eigvecs, 'col', split_axis=1, concat_axis=0, tiled=True)  127 us
    all_gather x1, waiting for transfers between devices, on_device(): gathered = lax.all_gather(panels, 'col', axis=2, tiled=True)  105 us
    dot_general x3, matrix products, spread(): lax.dot_general(panel_t, right, (((0,), (0,)), ((), ())), precision=lax.P...  54 us
    dot_general x6, matrix products, product(): jnp.dot(left, right, precision=lax.Precision.HIGHEST, preferred_element_t...  44.3 us
  transfers between devices with their start and end apart: 5, of which 5 were waited for; matrix products, arithmetic and copies ran while one was open for 1% of the time, Pallas kernels for 0%

commit v1 on v0

--- a/solution.py
+++ b/solution.py
@@ -43,7 +43,9 @@
     block_size = tri_factors.shape[1]
     count = tri_factors.shape[0]
     tiles = lax.all_to_all(eigvecs, "col", split_axis=1, concat_axis=0, tiled=True)
-    gathered = lax.all_gather(panels, "col", axis=2, tiled=True)
+    gathered = jnp.concatenate(
+        lax.all_to_all(jnp.stack([panels] * lax.axis_size("col")), "col", 0, 0), axis=2
+    )
     start = lax.axis_index("row") * tiles.shape[0]
     vectors = [shaped(gathered[index], start, (index + 1) * block_size) for index in range(count)]
     return apply_chain(tiles, vectors, tri_factors, tile_single)

time: 591 us -> 815 us (1.38)
  waiting for transfers between devices: 452 us -> 588 us
  other arithmetic: 0.02 us -> 39.9 us
  local copies, waits for them, and re-layouts: 14.5 us -> 52.2 us
  starting transfers between devices: 7.47 us -> 25.8 us
  matrix products: 98.3 us -> 87 us
    all_to_all x0 -> x1, waiting for transfers between devices: none -> 329 us  [on_device(): lax.all_to_all(jnp.stack([panels] * lax.axis_size('col')), 'col', 0, 0)]
    all_gather x1 -> x0, waiting for transfers between devices: 105 us -> none  [on_device(): gathered = lax.all_gather(panels, 'col', axis=2, tiled=True)]
    all_to_all x1, waiting for transfers between devices: 127 us -> 67.2 us  [on_device(): lax.all_to_all(eigvecs, 'col', split_axis=1, concat_axis=0, tiled=True)]
    psum x3, waiting for transfers between devices: 219 us -> 192 us  [tile_single(): return lax.psum(values, 'row')]
    all_to_all x0 -> x1, local copies, waits for them, and re-layouts: none -> 24.7 us  [on_device(): lax.all_to_all(jnp.stack([panels] * lax.axis_size('col')), 'col', 0, 0)]
    slice x0 -> x1, other arithmetic: none -> 20.9 us  [on_device(): gathered[index]]
    dot_general x3, matrix products: 54 us -> 33.7 us  [spread(): lax.dot_general(panel_t, right, (((0,), (0,)), ((), ())), precision=lax.P...]
    select_n x0 -> x1, other arithmetic: none -> 18.9 us  [shaped(): jnp.where(place < limit, jnp.float32(0.0), jnp.where(place == limit, jnp....]
  transfers between devices with their start and end apart: 5 -> 5, of which waited for: 5 -> 5; matrix products, arithmetic and copies ran while one was open for 1% -> 9% of each run, Pallas kernels for 0% -> 0%
where the time goes in v1:
time: 815 us; the launch traced here: 807 us
  waiting for transfers between devices  588 us (72%)
  matrix products  87 us (11%)
  local copies, waits for them, and re-layouts  52.2 us (6%)
  other arithmetic  39.9 us (5%)
  starting transfers between devices  25.8 us (3%)
  between operations  13.7 us (2%)
    all_to_all x1, waiting for transfers between devices, on_device(): lax.all_to_all(jnp.stack([panels] * lax.axis_size('col')), 'col', 0, 0)  329 us
    psum x3, waiting for transfers between devices, tile_single(): return lax.psum(values, 'row')  192 us
    all_to_all x1, waiting for transfers between devices, on_device(): lax.all_to_all(eigvecs, 'col', split_axis=1, concat_axis=0, tiled=True)  67.2 us
    dot_general x6, matrix products, product(): jnp.dot(left, right, precision=lax.Precision.HIGHEST, preferred_element_t...  53.3 us
    dot_general x3, matrix products, spread(): lax.dot_general(panel_t, right, (((0,), (0,)), ((), ())), precision=lax.P...  33.7 us
    all_to_all x1, local copies, waits for them, and re-layouts, on_device(): lax.all_to_all(jnp.stack([panels] * lax.axis_size('col')), 'col', 0, 0)  24.7 us
    slice x1, other arithmetic, on_device(): gathered[index]  20.9 us
    select_n x1, other arithmetic, shaped(): jnp.where(place < limit, jnp.float32(0.0), jnp.where(place == limit, jnp....  18.9 us
  transfers between devices with their start and end apart: 5, of which 5 were waited for; matrix products, arithmetic and copies ran while one was open for 9% of the time, Pallas kernels for 0%

profile of v1, /device:TPU:0, one launch (start us, length us, event | category | flops | bytes accessed | tf_op | source)
XLA Modules:
  0.0 806.8 jit_solution(5193026411162780381)
XLA Ops:
  6.5 13.0 %stack.2 = f32[16,3,256,512]{3,2,1,0:T(8,128)} broadcast(f32[3,256,512]{2,1,0:T(8,128)} %param.4), dimensions={1,2,3} | broadcast | bytes 26738688 | tf_op jit(solution)/shard_map/stack | solution.py:47
  19.5 7.2 all-to-all-start.1
  26.7 7.7 copy.10
  34.4 329.1 %all-to-all-done.1 = f32[16,3,256,512]{3,2,1,0:T(8,128)} async-done(((f32[16,3,256,512]{3,2,1,0:T(8,128)}), f32[16,3,256,512]{3,2,1,0:T(8,128)}, u32[]{:S(2)}, u32[]{:S(2)}) %all-to-all-start.1) | async-done | bytes 25165856 | tf_op jit(solution)/shard_map/all_to_all | solution.py:47
  363.5 6.3 all-to-all-start
  369.8 0.0 all-reduce.4.cloned.1.call-start
  369.9 24.7 %copy.7 = f32[16,3,256,512]{2,3,0,1:T(8,128)} copy(f32[16,3,256,512]{3,2,1,0:T(8,128)} %all-to-all-done.1) | data formatting | bytes 50331648 | tf_op jit(solution)/shard_map/all_to_all | solution.py:47
  394.6 20.9 %fusion.12 = (f32[1,256,16,512]{1,3,2,0:T(8,128)}, f32[1,256,16,512]{1,3,2,0:T(8,128)}, f32[1,256,16,512]{1,3,2,0:T(8,128)}, f32[1,256,16,512]{1,3,2,0:T(8,128)}) fusion(f32[3,256,16,512]{1,3,2,0:T(8,128)} %bitcast.47, s32[256]{0:T(256)S(1)} %iota_add_fusion.3, s32[16,512]{1,0:T(8,128)S(1)} %add_add_fusion), kind=kLoop, calls=%fused_computation.25 | loop fusion | flops 8388608 | bytes 58754048 | tf_op jit(solution)/shard_map/slice | solution.py:50
  415.5 67.2 %all-to-all-done = f32[512,16,256]{2,0,1:T(8,128)} async-done(((f32[512,16,256]{2,0,1:T(8,128)}), f32[512,16,256]{2,0,1:T(8,128)}, u32[]{:S(2)}, u32[]{:S(2)}) %all-to-all-start) | async-done | bytes 8388640 | tf_op jit(solution)/shard_map/all_to_all | solution.py:45
  482.8 17.7 %fusion.13 = f32[256,256]{1,0:T(8,128)} fusion(f32[256,8192]{0,1:T(8,128)} %bitcast.48, f32[8192,256]{1,0:T(8,128)} %bitcast.1), kind=kOutput, calls=%fused_computation.26 | convolution fusion | flops 6442450944 | bytes 17039360 | tf_op jit(solution)/shard_map/dot_general | solution.py:8
  500.5 0.0 all-reduce.4.cloned.1.call-update
  500.5 12.3 %all-reduce.6.cloned.1.call-start = ((), (), s32[]{:S(2)}) async-start(), calls=%async_computation.3 | async-start | bytes 524288 | tf_op jit(solution)/shard_map/psum | solution.py:39
  512.8 0.0 copy-start.2
  512.9 18.9 %fusion = (f32[256,8192]{0,1:T(8,128)}, f32[256,8192]{0,1:T(8,128)}, f32[256,8192]{0,1:T(8,128)}) fusion(f32[1,256,16,512]{1,3,2,0:T(8,128)} %get-tuple-element.5, s32[256]{0:T(256)S(1)} %get-tuple-element.12, s32[8192]{0:T(1024)S(1)} %iota_add_fusion, f32[1,256,16,512]{1,3,2,0:T(8,128)} %get-tuple-element.8, s32[256]{0:T(256)S(1)} %iota_add_fusion.3, ...), kind=kLoop, calls=%fused_computation.5 | loop fusion | flops 25165824 | bytes 50367488 | tf_op jit(solution)/shard_map/jit(_where)/select_n | solution.py:26
  531.7 44.4 %all-reduce.4.cloned.1.call-done = f32[256,256]{1,0:T(8,128)} async-done(((f32[256,256]{1,0:T(8,128)}), f32[256,256]{1,0:T(8,128)}) %all-reduce.4.cloned.1.call-update) | async-done | bytes 262160 | tf_op jit(solution)/shard_map/psum | solution.py:39
  576.2 0.0 copy-done.2
  576.2 0.0 slice-start
  576.2 1.7 fusion.7
  577.9 0.0 slice-start.1
  577.9 10.6 %convolution_subtract_fusion.2 = f32[8192,256]{1,0:T(8,128)S(1)} fusion(f32[8192,256]{1,0:T(8,128)} %bitcast.1, f32[256,8192]{0,1:T(8,128)} %get-tuple-element.10, f32[256,256]{1,0:T(8,128)S(1)} %fusion.7), kind=kOutput, calls=%fused_computation.2 | convolution fusion | flops 6444548096 | bytes 25427968 | tf_op jit(solution)/shard_map/dot_general | solution.py:12
  588.4 0.0 copy-start
  588.5 3.4 copy-done
  591.8 0.0 slice-done
  591.8 0.0 slice-done.1
  591.9 14.2 %fusion.14 = f32[256,256]{1,0:T(8,128)} fusion(f32[256,8192]{0,1:T(8,128)S(1)} %bitcast.46, f32[8192,256]{1,0:T(8,128)S(1)} %convolution_subtract_fusion.2), kind=kOutput, calls=%fused_computation.27 | convolution fusion | flops 6442450944 | bytes 17039360 | tf_op jit(solution)/shard_map/dot_general | solution.py:8
  606.1 0.0 all-reduce.6.cloned.1.call-update
  606.1 0.0 all-reduce.8.cloned.1.call-start
  606.2 73.7 %all-reduce.6.cloned.1.call-done = f32[256,256]{1,0:T(8,128)} async-done(((f32[256,256]{1,0:T(8,128)}), f32[256,256]{1,0:T(8,128)}) %all-reduce.6.cloned.1.call-update) | async-done | bytes 262160 | tf_op jit(solution)/shard_map/psum | solution.py:39
  679.8 1.5 fusion.5
  681.4 10.4 %convolution_subtract_fusion.1 = f32[8192,256]{1,0:T(8,128)S(1)} fusion(f32[8192,256]{1,0:T(8,128)} %copy-done, f32[256,8192]{0,1:T(8,128)} %get-tuple-element.11, f32[256,256]{1,0:T(8,128)S(1)} %fusion.5), kind=kOutput, calls=%fused_computation.1 | convolution fusion | flops 6444548096 | bytes 25427968 | tf_op jit(solution)/shard_map/dot_general | solution.py:12
  691.8 0.0 copy-start.1
  691.8 3.4 copy-done.1
  695.2 16.7 %fusion.15 = f32[256,256]{1,0:T(8,128)} fusion(f32[256,8192]{0,1:T(8,128)} %get-tuple-element.9, f32[8192,256]{1,0:T(8,128)S(1)} %convolution_subtract_fusion.1), kind=kOutput, calls=%fused_computation.28 | convolution fusion | flops 6442450944 | bytes 17039360 | tf_op jit(solution)/shard_map/dot_general | solution.py:8
  711.9 0.0 all-reduce.8.cloned.1.call-update
  711.9 73.7 %all-reduce.8.cloned.1.call-done = f32[256,256]{1,0:T(8,128)} async-done(((f32[256,256]{1,0:T(8,128)}), f32[256,256]{1,0:T(8,128)}) %all-reduce.8.cloned.1.call-update) | async-done | bytes 262160 | tf_op jit(solution)/shard_map/psum | solution.py:39
  785.6 1.5 fusion.3
  787.1 12.7 %convolution_subtract_fusion = f32[8192,256]{1,0:T(8,128)} fusion(f32[8192,256]{1,0:T(8,128)} %copy-done.1, f32[256,8192]{0,1:T(8,128)} %get-tuple-element.9, f32[256,256]{1,0:T(8,128)S(1)} %fusion.3), kind=kOutput, calls=%fused_computation | convolution fusion | flops 6444548096 | bytes 25427968 | tf_op jit(solution)/shard_map/dot_general | solution.py:12
  (5 shorter events, 0.0 us)
Async XLA Ops:
  19.5 344.0 %all-to-all-start.1 = ((f32[16,3,256,512]{3,2,1,0:T(8,128)}), f32[16,3,256,512]{3,2,1,0:T(8,128)}, u32[]{:S(2)}, u32[]{:S(2)}) async-start(f32[16,3,256,512]{3,2,1,0:T(8,128)} %stack.2), calls=%async_computation.1 | async-start | bytes 50331648 | tf_op jit(solution)/shard_map/all_to_all | solution.py:47
  363.5 119.3 %all-to-all-start = ((f32[512,16,256]{2,0,1:T(8,128)}), f32[512,16,256]{2,0,1:T(8,128)}, u32[]{:S(2)}, u32[]{:S(2)}) async-start(f32[512,16,256]{2,0,1:T(8,128)} %bitcast.49), calls=%async_computation | async-start | bytes 16777216 | tf_op jit(solution)/shard_map/all_to_all | solution.py:45
  369.8 206.4 %all-reduce.4.cloned.1.call-start = ((), (), s32[]{:S(2)}) async-start(), calls=%async_computation.2 | async-start | bytes 524288 | tf_op jit(solution)/shard_map/psum | solution.py:39
  500.5 179.3 %all-reduce.6.cloned.1.call-start = ((), (), s32[]{:S(2)}) async-start(), calls=%async_computation.3 | async-start | bytes 524288 | tf_op jit(solution)/shard_map/psum | solution.py:39
  512.8 63.3 %copy-start.2 = (f32[3,256,256]{2,1,0:T(8,128)S(1)}, f32[3,256,256]{2,1,0:T(8,128)}, u32[]{:S(2)}) copy-start(f32[3,256,256]{2,1,0:T(8,128)} %param.5) | copy-start | bytes 2359300
  576.2 15.7 %slice-start = ((s8[8388608]{0:T(1024)(128)(4,1)}), s8[4194304]{0:T(1024)(128)(4,1)S(1)}, s32[]{:S(2)}) async-start(s8[8388608]{0:T(1024)(128)(4,1)} %bitcast.45), calls=%async_computation.5 | async-start | bytes 8388608
  577.9 14.0 %slice-start.1 = ((s8[8388608]{0:T(1024)(128)(4,1)}), s8[4194304]{0:T(1024)(128)(4,1)S(1)}, s32[]{:S(2)}) async-start(s8[8388608]{0:T(1024)(128)(4,1)} %bitcast.45), calls=%async_computation.6 | async-start | bytes 8388608
  588.4 3.4 copy-start
  606.1 179.5 %all-reduce.8.cloned.1.call-start = ((), (), s32[]{:S(2)}) async-start(), calls=%async_computation.4 | async-start | bytes 524288 | tf_op jit(solution)/shard_map/psum | solution.py:39
  691.8 3.4 copy-start.1
Sparse Core Ops, SparseCore 0:
  500.6 75.4 all-reduce.3
  606.2 73.5 all-reduce.5
  712.0 73.5 all-reduce.7
